TPU v7x, 32 devices: a whole 2x2x4 slice. The times are simulated.
32 devices in a mesh: lat: 8 (over z, y), lon: 4 (over x, core).
Axes of the slice: x: 2, y: 2, z: 4, core: 2. Of those that a mesh axis runs over, the one named last changes fastest.
Arguments:
- prognostic: float32 [6, 2, 2304, 1024], P(None, None, 'lon', 'lat'), may hold values from -6 to 6
- wind_zonal: float32 [2, 1024], P(None, 'lat'), may hold values from -1 to 1
- wind_merid: float32 [2, 1024], P(None, 'lat'), may hold values from -0.5 to 0.5
- layer_depth: float32 [2], replicated, may hold values from 0.25 to 1
- diffusion: float32 [3, 2], replicated, may hold values from 0.05 to 0.4
Outputs:
- prognostic_out: float32 [6, 2, 2304, 1024], P(None, None, 'lon', 'lat')
All inputs are finite; a program needn't handle non-finite values.
Results may differ from a plain program's by a relative error of at most 0.00013.
Values sent between devices are 32-bit elements; how exact they have to be, the bound alone decides.
A program may use at most 128 MiB of HBM per device.

v0:
```python
import math

import jax
import jax.numpy as jnp
import ml_dtypes
import numpy as np
from jax import lax
from jax.experimental import pallas as pl
from jax.experimental.pallas import tpu as pltpu
from jax.sharding import PartitionSpec as P

ITERS = 3


time_step = 0.15
highest = lax.Precision.HIGHEST


def with_halo(block, sides, width, periodic):
    for axis, dim in sides:
        count = lax.axis_size(axis)
        forward = [(i, i + 1) for i in range(count - 1)]
        if periodic:
            forward.append((count - 1, 0))
        backward = [(target, source) for source, target in forward]
        low = lax.ppermute(
            lax.slice_in_dim(block, block.shape[dim] - width, None, axis=dim), axis, forward
        )
        high = lax.ppermute(lax.slice_in_dim(block, 0, width, axis=dim), axis, backward)
        block = jnp.concatenate([low, block, high], axis=dim)
    return block


def latitude(row_ids, lat_total):
    return (row_ids.astype(jnp.float32) + 0.5) * (math.pi / lat_total) - 0.5 * math.pi


def damping(row_ids, lat_total, circle_len):
    cos_ratio = jnp.cos(latitude(row_ids, lat_total)) / math.cos(0.25 * math.pi)
    wave_ids = jnp.arange(circle_len // 2 + 1)
    sine_vals = jnp.sin(wave_ids.astype(jnp.float32) * (math.pi / circle_len))
    safe_sines = jnp.where(wave_ids == 0, 1.0, sine_vals)
    return jnp.where(
        wave_ids[None, :] == 0, 1.0, jnp.minimum(1.0, cos_ratio[:, None] / safe_sines[None, :])
    )


def tendency(
    fields_now,
    north_rows,
    south_rows,
    east_cols,
    west_cols,
    row_ids,
    lat_total,
    wind_zonal,
    wind_merid,
    layer_depth,
    diffusion,
):
    latitudes = latitude(row_ids, lat_total)
    cos_centre = jnp.cos(latitudes)
    cos_north = jnp.cos(latitude(row_ids + 1, lat_total))
    cos_south = jnp.cos(latitude(row_ids - 1, lat_total))
    coriolis = jnp.sin(latitudes)
    zonal_diff = (east_cols - west_cols) / (2.0 * cos_centre)
    merid_diff = 0.5 * (north_rows - south_rows)
    advect = wind_zonal[:, None, :] * zonal_diff + wind_merid[:, None, :] * merid_diff
    diverge = zonal_diff[0] + (north_rows[1] * cos_north - south_rows[1] * cos_south) / (
        2.0 * cos_centre
    )
    zonal_tend = -advect[0] + coriolis * fields_now[1] - zonal_diff[2]
    merid_tend = -advect[1] - coriolis * fields_now[0] - merid_diff[2]
    height_tend = -advect[2] - layer_depth[:, None, None] * diverge
    tracer_tend = -advect[3:] + diffusion[:, :, None, None] * (
        north_rows[3:] - 2.0 * fields_now[3:] + south_rows[3:]
    )
    return jnp.concatenate(
        [zonal_tend[None], merid_tend[None], height_tend[None], tracer_tend], axis=0
    )


def split_length(total):
    first = int(math.isqrt(total))
    while total % first != 0:
        first = first - 1
    return (first, total // first)


def trig_table(length):
    counts = jnp.arange(length, dtype=jnp.int32)
    phases = counts[:, None] * counts[None, :] % length
    angles = phases.astype(jnp.float32) * (2.0 * math.pi / length)
    return (jnp.cos(angles), jnp.sin(angles))


def twist_table(outer, inner, total):
    outer_ids = jnp.arange(outer, dtype=jnp.int32)
    inner_ids = jnp.arange(inner, dtype=jnp.int32)
    angles = (outer_ids[:, None] * inner_ids[None, :] % total).astype(jnp.float32) * (
        2.0 * math.pi / total
    )
    return (jnp.cos(angles)[None], jnp.sin(angles)[None])


def forward_real(signal):
    vectors, total = signal.shape
    inner, outer = split_length(total)
    grid = signal.reshape(vectors, outer, inner)
    cos_outer, sin_outer = trig_table(outer)
    first_re = jnp.einsum("mba,bk->mka", grid, cos_outer, precision=highest)
    first_im = -jnp.einsum("mba,bk->mka", grid, sin_outer, precision=highest)
    twist_cos, twist_sin = twist_table(outer, inner, total)
    mid_re = first_re * twist_cos + first_im * twist_sin
    mid_im = first_im * twist_cos - first_re * twist_sin
    cos_inner, sin_inner = trig_table(inner)
    last_re = jnp.einsum("mka,aq->mqk", mid_re, cos_inner, precision=highest) + jnp.einsum(
        "mka,aq->mqk", mid_im, sin_inner, precision=highest
    )
    last_im = jnp.einsum("mka,aq->mqk", mid_im, cos_inner, precision=highest) - jnp.einsum(
        "mka,aq->mqk", mid_re, sin_inner, precision=highest
    )
    return (last_re.reshape(vectors, total), last_im.reshape(vectors, total))


def inverse_real(spec_re, spec_im):
    vectors, total = spec_re.shape
    inner, outer = split_length(total)
    grid_re = spec_re.reshape(vectors, outer, inner)
    grid_im = spec_im.reshape(vectors, outer, inner)
    cos_outer, sin_outer = trig_table(outer)
    first_re = jnp.einsum("mba,bk->mka", grid_re, cos_outer, precision=highest) - jnp.einsum(
        "mba,bk->mka", grid_im, sin_outer, precision=highest
    )
    first_im = jnp.einsum("mba,bk->mka", grid_im, cos_outer, precision=highest) + jnp.einsum(
        "mba,bk->mka", grid_re, sin_outer, precision=highest
    )
    twist_cos, twist_sin = twist_table(outer, inner, total)
    mid_re = first_re * twist_cos - first_im * twist_sin
    mid_im = first_im * twist_cos + first_re * twist_sin
    cos_inner, sin_inner = trig_table(inner)
    last_re = jnp.einsum("mka,aq->mqk", mid_re, cos_inner, precision=highest) - jnp.einsum(
        "mka,aq->mqk", mid_im, sin_inner, precision=highest
    )
    return last_re.reshape(vectors, total)


def local(prognostic, wind_zonal, wind_merid, layer_depth, diffusion):
    field_count, level_count, col_count, row_count = prognostic.shape
    lat_devs = lax.axis_size("lat")
    lon_devs = lax.axis_size("lon")
    lat_total = row_count * lat_devs
    circle_len = col_count * lon_devs
    lat_pos = lax.axis_index("lat")
    lon_pos = lax.axis_index("lon")
    row_ids = lat_pos * row_count + jnp.arange(row_count, dtype=jnp.int32)
    quarter = lat_devs // 4
    is_polar = (lat_pos < quarter) | (lat_pos >= lat_devs - quarter)

    def smooth(sector, start_row):
        vectors, total, slab_rows = sector.shape
        halfway = damping(start_row + jnp.arange(slab_rows, dtype=jnp.int32), lat_total, circle_len)
        mirrored = halfway[:, 1 : circle_len // 2][:, ::-1]
        factors = jnp.concatenate([halfway, mirrored], axis=1)[None]
        rows_last = jnp.transpose(sector, (0, 2, 1)).reshape(vectors * slab_rows, total)
        spec_re, spec_im = forward_real(rows_last)
        spec_re = (spec_re.reshape(vectors, slab_rows, total) * factors).reshape(
            vectors * slab_rows, total
        )
        spec_im = (spec_im.reshape(vectors, slab_rows, total) * factors).reshape(
            vectors * slab_rows, total
        )
        back = inverse_real(spec_re, spec_im) * (1.0 / circle_len)
        return jnp.transpose(back.reshape(vectors, slab_rows, total), (0, 2, 1))

    fields_now = prognostic
    for substep in range(ITERS):
        lat_padded = with_halo(fields_now, (("lat", 3),), 1, False)
        lon_padded = with_halo(fields_now, (("lon", 2),), 1, True)
        tendency_now = tendency(
            fields_now,
            lat_padded[:, :, :, 2:],
            lat_padded[:, :, :, :-2],
            lon_padded[:, :, 2:],
            lon_padded[:, :, :-2],
            row_ids,
            lat_total,
            wind_zonal,
            wind_merid,
            layer_depth,
            diffusion,
        )
        flattened = tendency_now.reshape(field_count * level_count, col_count, row_count)

        def filter_sector(sector):
            slab_rows = sector.shape[2]
            start_row = lat_pos * row_count + lon_pos * slab_rows
            damped = lax.cond(
                is_polar, lambda inner: smooth(inner, start_row), lambda inner: inner, sector
            )
            return lax.all_to_all(damped, "lon", split_axis=1, concat_axis=2, tiled=True)

        filtered = filter_sector(
            lax.all_to_all(flattened, "lon", split_axis=2, concat_axis=1, tiled=True)
        )
        fields_now = fields_now + time_step * filtered.reshape(fields_now.shape)
    return fields_now


HALO = 3
BLOCK = 32
FOLD = 8
MESH = pl.DeviceIdType.MESH


def wave_layout(total):
    q = total // 4
    pad_a = -(-(q // 2 + 1) // 32) * 32
    wave_a = np.full(pad_a, -1)
    wave_a[: q // 2 + 1] = 4 * np.arange(q // 2 + 1)
    wave_b = 4 * np.arange(q // 2) + 2
    wave_c = 2 * np.arange(q) + 1
    return wave_a, wave_b, wave_c


def split_bf16(table):
    table = table.astype(np.float32)
    high = table.astype(ml_dtypes.bfloat16)
    low = (table - high.astype(np.float32)).astype(ml_dtypes.bfloat16)
    return np.stack([high, low])


def wave_tables(total):
    out_fwd, out_inv = [], []
    for waves, width in zip(wave_layout(total), (total // 4, total // 4, total // 2)):
        angle = 2 * np.pi * (waves[:, None] * np.arange(width)[None, :] % total) / total
        real = waves >= 0
        cos = np.where(real[:, None], np.cos(angle), 0.0)
        sin = np.where(real[:, None], np.sin(angle), 0.0)
        weight = np.where((waves == 0) | (2 * waves == total), 1.0, 2.0)[:, None] / total
        out_fwd.append(split_bf16(np.concatenate([cos, -sin], axis=0)))
        out_inv.append(split_bf16(np.concatenate([cos * weight, -sin * weight], axis=0).T))
    return out_fwd, out_inv


def wave_vectors(total):
    waves = np.concatenate(wave_layout(total))
    sigma = np.where(waves >= 0, np.sin(2 * np.pi * waves / total), 0.0)
    sine = np.where(waves > 0, np.sin(np.pi * waves / total), 1.0)
    inverse = np.where(waves == 0, 1e30, 1.0 / sine)
    return np.stack([sigma, inverse]).astype(np.float32)


def geometry(row_ids, lat_total):
    def lat(ids):
        step = np.float32(math.pi / lat_total)
        return ((ids.astype(np.float32) + np.float32(0.5)) * step - np.float32(0.5 * math.pi)).astype(np.float64)

    cos_c = np.cos(lat(row_ids))
    valid = (row_ids >= 0) & (row_ids < lat_total)
    rows = [
        1.0 / cos_c,
        np.sin(lat(row_ids)),
        0.5 * np.cos(lat(row_ids + 1)) / cos_c,
        0.5 * np.cos(lat(row_ids - 1)) / cos_c,
        np.abs(cos_c) / math.cos(0.25 * math.pi),
        np.where(valid, time_step, 0.0),
    ]
    return np.stack(rows + [np.zeros_like(cos_c)] * 2).astype(np.float32)


def geometry_tables(lat_devs, row_count):
    total = lat_devs * row_count
    mains, edges = [], []
    keep = HALO - 1
    offsets = np.concatenate([np.arange(-HALO, keep), np.arange(-keep, HALO) + row_count])
    for pos in range(lat_devs):
        mains.append(geometry(pos * row_count + np.arange(row_count), total))
        short = geometry(pos * row_count + offsets, total)
        wide = np.zeros((8, 128), np.float32)
        for v in range(3):
            wide[:, BLOCK * v : BLOCK * v + len(offsets)] = short
        edges.append(wide)
    return np.stack(mains), np.stack(edges)


def roll(x, shift):
    return pltpu.roll(x, shift % 128, 1)


def substeps(state, edge, sigma, inv_sine, mc, ec):
    lane = lax.broadcasted_iota(jnp.int32, edge[0].shape, 1)
    first, last = lane == 0, lane == 127
    fac = mc(17) * jnp.minimum(1.0, mc(16) * inv_sine)
    efac = ec(12) * jnp.minimum(1.0, ec(11) * inv_sine)
    for step in range(ITERS):
        tends, zons, etend, ezon = [], [], [], []
        for part in range(2):
            a = [state[v][part] for v in range(3)]
            h = edge[part]
            east = [jnp.where(last, roll(h, 120 - BLOCK * v), roll(a[v], 127)) for v in range(3)]
            west = [jnp.where(first, roll(h, 126 - BLOCK * v), roll(a[v], 1)) for v in range(3)]
            t = [mc(v) * east[v] + mc(3 + v) * west[v] + mc(6 + v) * a[v] for v in range(3)]
            t[0] = t[0] + mc(9) * a[1]
            t[1] = t[1] - mc(9) * a[0] - mc(10) * (east[2] - west[2])
            t[2] = t[2] + mc(11) * east[1] + mc(12) * west[1]
            z = [mc(13) * a[v] for v in range(3)]
            z[0] = z[0] + mc(14) * a[2]
            z[2] = z[2] + mc(15) * a[0]
            tends.append(t)
            zons.append(z)
            if step < ITERS - 1:
                etend.append(
                    ec(0) * roll(h, 127) + ec(1) * roll(h, 1) + ec(2) * h
                    + ec(3) * roll(h, -BLOCK) + ec(4) * roll(h, BLOCK)
                    + ec(5) * roll(h, -BLOCK - 1) + ec(6) * roll(h, -BLOCK + 1)
                    + ec(7) * roll(h, BLOCK - 1) + ec(8) * roll(h, BLOCK + 1)
                )
                ezon.append(ec(9) * h + ec(10) * roll(h, 64))
        state = [
            (
                state[v][0] + fac * (tends[0][v] + sigma * zons[1][v]),
                state[v][1] + fac * (tends[1][v] - sigma * zons[0][v]),
            )
            for v in range(3)
        ]
        if step < ITERS - 1:
            edge = (
                edge[0] + efac * (etend[0] + sigma * ezon[1]),
                edge[1] + efac * (etend[1] - sigma * ezon[0]),
            )
    return state


def wave_kernel(
    x_ref, wz_ref, wm_ref, depth_ref, kappa_ref, gm_ref, ge_ref, kv_ref,
    fa_h, fb_h, fc_h, ia_h, ib_h, ic_h, out_ref,
    fa, fb, fc, ia, ib, ic, recv, home, xh, xl, xs, sre, sim, sh, sl, ss,
    wind, wind_in, up, down, from_low, from_high, mc_ref, ec_ref,
    table_sem, own_sem, go_send, go_recv, back_send, back_recv, wind_send, wind_recv, edge_send, edge_recv,
):
    lat, lon = lax.axis_index("lat"), lax.axis_index("lon")
    lat_devs = lax.axis_size("lat")
    quarter = recv.shape[2]
    ka, kb, kc = fa.shape[1] // 2, fb.shape[1] // 2, fc.shape[1] // 2
    waves = ka + kb + kc
    has_low, has_high = lat > 0, lat < lat_devs - 1
    kind, level = lon // 2, lon % 2

    barrier = pltpu.get_barrier_semaphore()
    for p in (1, 2, 3):
        pl.semaphore_signal(barrier, inc=1, device_id=(lat, (lon + p) % 4), device_id_type=MESH)

    @pl.when(has_low)
    def _():
        pl.semaphore_signal(barrier, inc=1, device_id=(lat - 1, lon), device_id_type=MESH)

    @pl.when(has_high)
    def _():
        pl.semaphore_signal(barrier, inc=1, device_id=(lat + 1, lon), device_id_type=MESH)

    pl.semaphore_wait(barrier, 3 + jnp.where(has_low, 1, 0) + jnp.where(has_high, 1, 0))

    def go(p, v):
        to = (lon + p) % 4
        return pltpu.make_async_remote_copy(
            src_ref=x_ref.at[3 * (to // 2) + v, to % 2], dst_ref=recv.at[p, v],
            send_sem=go_send.at[p, v], recv_sem=go_recv.at[p, v],
            device_id=(lat, to), device_id_type=MESH,
        )

    def back(p, v):
        to = (lon + p) % 4
        return pltpu.make_async_remote_copy(
            src_ref=home.at[to, v], dst_ref=out_ref.at[3 * kind + v, level],
            send_sem=back_send.at[p, v], recv_sem=back_recv.at[p, v],
            device_id=(lat, to), device_id_type=MESH,
        )

    def own_in(v):
        return pltpu.make_async_copy(x_ref.at[3 * kind + v, level], recv.at[0, v], own_sem.at[0, v])

    def own_out(v):
        return pltpu.make_async_copy(home.at[lon, v], out_ref.at[3 * kind + v, level], own_sem.at[1, v])

    def beside(src, dst, side, send_sem, recv_sem):
        return pltpu.make_async_remote_copy(
            src_ref=src, dst_ref=dst, send_sem=send_sem.at[side], recv_sem=recv_sem.at[side],
            device_id=((lat + (1 if side == 0 else lat_devs - 1)) % lat_devs, lon), device_id_type=MESH,
        )

    for v in range(3):
        for p in (2, 1, 3):
            go(p, v).start()
        own_in(v).start()
    tables = [
        pltpu.make_async_copy(src, dst, table_sem.at[i])
        for i, (src, dst) in enumerate(
            ((fa_h, fa), (fb_h, fb), (fc_h, fc), (ia_h, ia), (ib_h, ib), (ic_h, ic))
        )
    ]
    for t in tables:
        t.start()

    wind[0:2, :] = wz_ref[...]
    wind[2:4, :] = wm_ref[...]
    wind[4:8, :] = jnp.zeros((4, 128), jnp.float32)
    up_wind = lambda: beside(wind, wind_in.at[0], 0, wind_send, wind_recv)
    down_wind = lambda: beside(wind, wind_in.at[1], 1, wind_send, wind_recv)
    up_edge = lambda: beside(up, from_low, 0, edge_send, edge_recv)
    down_edge = lambda: beside(down, from_high, 1, edge_send, edge_recv)

    @pl.when(has_high)
    def _():
        up_wind().start()

    @pl.when(has_low)
    def _():
        down_wind().start()

    @pl.when(jnp.logical_not(has_low))
    def _():
        wind_in[0] = jnp.zeros((8, 128), jnp.float32)
        from_low[...] = jnp.zeros(from_low.shape, jnp.float32)

    @pl.when(jnp.logical_not(has_high))
    def _():
        wind_in[1] = jnp.zeros((8, 128), jnp.float32)
        from_high[...] = jnp.zeros(from_high.shape, jnp.float32)

    @pl.when(has_high)
    def _():
        up_wind().wait_send()
        down_wind().wait_recv()

    @pl.when(has_low)
    def _():
        down_wind().wait_send()
        up_wind().wait_recv()

    lane8 = lax.broadcasted_iota(jnp.int32, (8, 128), 1)
    spot8, block8 = lane8 % BLOCK, lane8 // BLOCK
    dyn = jnp.where(lon < 2, 1.0, 0.0).astype(jnp.float32)
    depth = depth_ref[level] * dyn
    kappa = [kappa_ref[v, level] * (1.0 - dyn) for v in range(3)]
    row = lambda ref, r: ref[lat, r : r + 1, :]
    wz, wm = wind[pl.ds(level, 1), :], wind[pl.ds(2 + level, 1), :]
    one = jnp.ones((1, 128), jnp.float32)
    inv, rot, cn, cs = (row(gm_ref, r) for r in range(4))
    coefs = (
        [kappa[v] - 0.5 * wm for v in range(3)] + [kappa[v] + 0.5 * wm for v in range(3)]
        + [-2.0 * kappa[v] * one for v in range(3)]
        + [dyn * rot, 0.5 * dyn * one, -depth * cn, depth * cs, wz * inv, dyn * inv, depth * inv, row(gm_ref, 4), row(gm_ref, 5)]
    )
    for r, c in enumerate(coefs):
        mc_ref[r : r + 1, :] = c

    below = jnp.where(lane8 >= 128 - HALO, wind_in[0], wind[...])
    above = jnp.where(lane8 < HALO, wind_in[1], wind[...])
    ewind = jnp.zeros((8, 128), jnp.float32)
    for v in range(3):
        val = jnp.where(spot8 < 5, roll(below, BLOCK * v + 3), roll(above, BLOCK * v + 7))
        ewind = jnp.where(block8 == v, val, ewind)
    used = (spot8 < 10) & (block8 < 3)
    ewind = jnp.where(used, ewind, 0.0)
    ec_ref[0:8, :] = ewind
    ez, em = ec_ref[pl.ds(level, 1), :], ec_ref[pl.ds(2 + level, 1), :]
    block = block8[0:1]
    only = lambda v, val: jnp.where(block == v, val, 0.0)
    ekap = only(0, kappa[0] * one) + only(1, kappa[1] * one) + only(2, kappa[2] * one)
    inv, rot, cn, cs = (row(ge_ref, r) for r in range(4))
    coefs = [
        ekap - 0.5 * em, ekap + 0.5 * em, -2.0 * ekap,
        only(0, dyn * rot), only(1, -dyn * rot), only(1, -0.5 * dyn * one), only(1, 0.5 * dyn * one),
        only(2, -depth * cn), only(2, depth * cs), ez * inv, only(0, dyn * inv) + only(2, depth * inv),
        row(ge_ref, 4), row(ge_ref, 5),
    ]
    for r, c in enumerate(coefs):
        ec_ref[r : r + 1, :] = c

    rows = 16
    slots = [(lon - s + 4) % 4 for s in range(4)]

    def split_in(v):
        @pl.loop(0, quarter // rows)
        def _(i):
            at = pl.ds(pl.multiple_of(i * rows, rows), rows)
            x = [recv[slots[s], v, at, :] for s in range(4)]
            y0, y1 = x[0] + x[2], x[1] + x[3]
            for part, val in enumerate((y0 + y1, y0 - y1, x[0] - x[2], x[1] - x[3])):
                high = val.astype(jnp.bfloat16)
                low = (val - high.astype(jnp.float32)).astype(jnp.bfloat16)
                to = pl.ds(pl.multiple_of(part * quarter + i * rows, rows), rows)
                if v < 2:
                    xh[to, v * 128 : v * 128 + 128] = high
                    xl[to, v * 128 : v * 128 + 128] = low
                else:
                    xs[to, 0:128] = high
                    xs[to, 128:256] = low

    dot = lambda p, q: jnp.dot(p, q, preferred_element_type=jnp.float32)

    def pair(top, bottom, high, low):
        return dot(top, high) + dot(bottom, high) + dot(top, low)

    def single(top, bottom, both):
        full = dot(top, both)
        return full[:, :128] + full[:, 128:] + dot(bottom, both[:, :128])

    def forward(lanes, product):
        for table, half, base, start, size in (
            (fa, ka, 0, 0, quarter), (fb, kb, ka, quarter, quarter), (fc, kc, ka + kb, 2 * quarter, 2 * quarter)
        ):
            src = slice(start, start + size)
            piece = half if half <= 320 else half // 2
            for dest, shift in ((sre, 0), (sim, half)):
                for p in range(0, half, piece):
                    at = slice(shift + p, shift + p + piece)
                    dest[base + p : base + p + piece, lanes] = product(table[0, at, :], table[1, at, :], src)

    def arrived(v):
        for p in (1, 2, 3):
            go(p, v).wait_recv()
        own_in(v).wait()

    arrived(0)
    split_in(0)
    arrived(1)
    split_in(1)
    for t in tables[:3]:
        t.wait()
    forward(slice(0, 256), lambda top, bottom, src: pair(top, bottom, xh[src, :], xl[src, :]))
    arrived(2)
    split_in(2)
    forward(slice(256, 384), lambda top, bottom, src: single(top, bottom, xs[src, :]))

    lane = lax.broadcasted_iota(jnp.int32, (8, 128), 1)
    spot, blk = lane % BLOCK, lane // BLOCK
    span = 4 * FOLD

    @pl.loop(0, waves // span)
    def _(i):
        ups = jnp.zeros((8, 128), jnp.float32)
        downs = ups
        for f in range(FOLD):
            at = pl.ds(pl.multiple_of(i * span + (f // 2) * 8, 8), 8)
            src = (sre, sim)[f % 2]
            here = (spot >= 3 * f) & (spot < 3 * f + 3)
            for v in range(3):
                a = src[at, v * 128 : v * 128 + 128]
                mask = here & (blk == v)
                ups = jnp.where(mask, roll(a, BLOCK * v + 3 * f + 3), ups)
                downs = jnp.where(mask, roll(a, BLOCK * v + 3 * f), downs)
        to = pl.ds(pl.multiple_of(i * 8, 8), 8)
        up[to, :] = ups
        down[to, :] = downs

    @pl.when(has_high)
    def _():
        up_edge().start()

    @pl.when(has_low)
    def _():
        down_edge().start()

    @pl.when(has_high)
    def _():
        up_edge().wait_send()
        down_edge().wait_recv()

    @pl.when(has_low)
    def _():
        down_edge().wait_send()
        up_edge().wait_recv()

    mc = lambda r: mc_ref[r : r + 1, :]
    ec = lambda r: ec_ref[r : r + 1, :]

    @pl.loop(0, waves // span)
    def _(i):
        packs = pl.ds(pl.multiple_of(i * 8, 8), 8)
        lows, highs = from_low[packs, :], from_high[packs, :]
        done = []
        for chunk in range(4):
            at = pl.ds(pl.multiple_of(i * span + chunk * 8, 8), 8)
            state = [
                (sre[at, v * 128 : v * 128 + 128], sim[at, v * 128 : v * 128 + 128]) for v in range(3)
            ]
            edge = []
            for part in range(2):
                f = 2 * chunk + part
                tile = jnp.where(spot < 3, roll(lows, -3 * f), roll(highs, 7 - 3 * f))
                for v in range(3):
                    a = state[v][part]
                    mine = jnp.where(spot < 5, roll(a, BLOCK * v + 3), roll(a, BLOCK * v + 7))
                    tile = jnp.where((blk == v) & (spot >= 3) & (spot < 7), mine, tile)
                edge.append(jnp.where((spot < 10) & (blk < 3), tile, 0.0))
            done.append(substeps(state, tuple(edge), kv_ref[0, at, :], kv_ref[1, at, :], mc, ec))
            if chunk % 2 == 0:
                continue
            to = pl.ds(pl.multiple_of(i * span + (chunk - 1) * 8, 16), 16)
            for v in range(3):
                for part in range(2):
                    val = jnp.concatenate([done[chunk - 1][v][part], done[chunk][v][part]], axis=0)
                    high = val.astype(jnp.bfloat16)
                    low = (val - high.astype(jnp.float32)).astype(jnp.bfloat16)
                    if v < 2:
                        sh[part, to, v * 128 : v * 128 + 128] = high
                        sl[part, to, v * 128 : v * 128 + 128] = low
                    else:
                        ss[part, to, 0:128] = high
                        ss[part, to, 128:256] = low

    for t in tables[3:]:
        t.wait()

    def inverse(product, vectors):
        def sums(table, base, half, at):
            out = None
            for part in range(2):
                cols = slice(part * half, part * half + half)
                term = product(table[0, at, cols], table[1, at, cols], part, slice(base, base + half))
                out = term if out is None else out + term
            return out

        piece = 192
        for p in range(0, quarter, piece):
            at = slice(p, p + piece)
            ya, yb = sums(ia, 0, ka, at), sums(ib, ka, kb, at)
            y0, y1 = ya + yb, ya - yb
            o0 = sums(ic, ka + kb, kc, at)
            o1 = sums(ic, ka + kb, kc, slice(quarter + p, quarter + p + piece))
            for n, v in enumerate(vectors):
                lanes = slice(n * 128, n * 128 + 128)
                for s, val in enumerate((y0 + o0, y1 + o1, y0 - o0, y1 - o1)):
                    home[s, v, at, :] = val[:, lanes]

    def send(v):
        for p in (2, 1, 3):
            back(p, v).start()
        own_out(v).start()

    inverse(lambda top, bottom, part, src: single(top, bottom, ss[part, src, :]), (2,))
    send(2)
    inverse(lambda top, bottom, part, src: pair(top, bottom, sh[part, src, :], sl[part, src, :]), (0, 1))
    send(0)
    send(1)
    for v in range(3):
        own_out(v).wait()
        for p in (1, 2, 3):
            go(p, v).wait_send()
            back(p, v).wait()


def local_waves(prognostic, wind_zonal, wind_merid, layer_depth, diffusion):
    col_count, row_count = prognostic.shape[2:]
    total = col_count * 4
    fwd, bwd = wave_tables(total)
    vectors = wave_vectors(total)
    waves = vectors.shape[1]
    vectors = np.ascontiguousarray(np.broadcast_to(vectors[:, :, None], (2, waves, 128)))
    mains, edges = geometry_tables(lax.axis_size("lat"), row_count)
    tables = [jnp.asarray(t) for t in fwd + bwd]
    bf16, f32 = jnp.bfloat16, jnp.float32
    vmem = pl.BlockSpec(memory_space=pltpu.VMEM)
    smem = pl.BlockSpec(memory_space=pltpu.SMEM)
    hbm = pl.BlockSpec(memory_space=pl.ANY)
    dma = pltpu.SemaphoreType.DMA
    return pl.pallas_call(
        wave_kernel,
        out_shape=jax.ShapeDtypeStruct(prognostic.shape, f32),
        in_specs=[hbm, vmem, vmem, smem, smem, vmem, vmem, vmem] + [hbm] * 6,
        out_specs=hbm,
        scratch_shapes=[pltpu.VMEM(t.shape, bf16) for t in tables] + [
            pltpu.VMEM((4, 3, col_count, row_count), f32),
            pltpu.VMEM((4, 3, col_count, row_count), f32),
            pltpu.VMEM((total, 256), bf16),
            pltpu.VMEM((total, 256), bf16),
            pltpu.VMEM((total, 256), bf16),
            pltpu.VMEM((waves, 384), f32),
            pltpu.VMEM((waves, 384), f32),
            pltpu.VMEM((2, waves, 256), bf16),
            pltpu.VMEM((2, waves, 256), bf16),
            pltpu.VMEM((2, waves, 256), bf16),
            pltpu.VMEM((8, 128), f32),
            pltpu.VMEM((2, 8, 128), f32),
            pltpu.VMEM((waves // 4, 128), f32),
            pltpu.VMEM((waves // 4, 128), f32),
            pltpu.VMEM((waves // 4, 128), f32),
            pltpu.VMEM((waves // 4, 128), f32),
            pltpu.VMEM((24, 128), f32),
            pltpu.VMEM((16, 128), f32),
            dma((6,)), dma((2, 3)), dma((4, 3)), dma((4, 3)), dma((4, 3)), dma((4, 3)),
            dma((2,)), dma((2,)), dma((2,)), dma((2,)),
        ],
        compiler_params=pltpu.CompilerParams(
            vmem_limit_bytes=58 * 2**20, collective_id=0, has_side_effects=True
        ),
        name="waves",
    )(prognostic, wind_zonal, wind_merid, layer_depth, diffusion, jnp.asarray(mains), jnp.asarray(edges),
      jnp.asarray(vectors), *tables)


def solution(mesh):
    return jax.shard_map(
        local_waves if mesh.shape["lon"] == 4 else local,
        mesh=mesh,
        in_specs=(P(None, None, "lon", "lat"), P(None, "lat"), P(None, "lat"), P(), P()),
        out_specs=P(None, None, "lon", "lat"),
        check_vma=False,
    )
```

profile of v0, /device:TPU:9, one launch (start us, length us, event | category | flops | bytes accessed | tf_op | source)
XLA Modules:
  0.0 148.6 jit_solution(2658828136067514672)
XLA Ops:
  0.0 1.3 copy.15.kappa_ref
  1.3 143.2 %waves.1 = f32[6,2,576,128]{3,2,1,0:T(8,128)} custom-call(f32[6,2,576,128]{3,2,1,0:T(8,128)} %x_ref.1, f32[2,128]{1,0:T(2,128)} %wz_ref.1, f32[2,128]{1,0:T(2,128)} %wm_ref.1, f32[2]{0:T(128)} %depth_ref.1, f32[3,2]{1,0:T(4,128)} %copy.15.kappa_ref, f32[8,8,128]{2,1,0:T(8,128)} %constant.24.clone.gm_ref, f32[8,8,128]{2,1,0:T(8,128)} %constant.25.clone.ge_ref, ...), custom_call_target="tpu_custom_call" | custom-call | tf_op jit(solution)/shard_map/waves/pallas_call | solution.py:669
  144.6 4.0 %copy.17 = f32[6,2,576,128]{3,2,1,0:T(8,128)} copy(f32[6,2,576,128]{3,2,1,0:T(8,128)} %waves.1) | data formatting | bytes 7077888
where the time goes:
time: 149 us
  Pallas kernels  143 us (96%)
  local copies, waits for them, and re-layouts  5.36 us (4%)
    pallas_call x1, Pallas kernels, local_waves(): pl.pallas_call(wave_kernel, out_shape=jax.ShapeDtypeStruct(prognostic.sha...  143 us
    unnamed x2, local copies, waits for them, and re-layouts  5.36 us

commit v1 on v0

--- a/solution.py
+++ b/solution.py
@@ -512,11 +512,9 @@
             (fa, ka, 0, 0, quarter), (fb, kb, ka, quarter, quarter), (fc, kc, ka + kb, 2 * quarter, 2 * quarter)
         ):
             src = slice(start, start + size)
-            piece = half if half <= 320 else half // 2
-            for dest, shift in ((sre, 0), (sim, half)):
-                for p in range(0, half, piece):
-                    at = slice(shift + p, shift + p + piece)
-                    dest[base + p : base + p + piece, lanes] = product(table[0, at, :], table[1, at, :], src)
+            full = product(table[0], table[1], src)
+            sre[base : base + half, lanes] = full[:half]
+            sim[base : base + half, lanes] = full[half:]
 
     def arrived(v):
         for p in (1, 2, 3):
@@ -615,25 +613,22 @@
         t.wait()
 
     def inverse(product, vectors):
-        def sums(table, base, half, at):
+        def sums(table, base, half):
             out = None
             for part in range(2):
                 cols = slice(part * half, part * half + half)
-                term = product(table[0, at, cols], table[1, at, cols], part, slice(base, base + half))
+                term = product(table[0, :, cols], table[1, :, cols], part, slice(base, base + half))
                 out = term if out is None else out + term
             return out
 
-        piece = 192
-        for p in range(0, quarter, piece):
-            at = slice(p, p + piece)
-            ya, yb = sums(ia, 0, ka, at), sums(ib, ka, kb, at)
-            y0, y1 = ya + yb, ya - yb
-            o0 = sums(ic, ka + kb, kc, at)
-            o1 = sums(ic, ka + kb, kc, slice(quarter + p, quarter + p + piece))
-            for n, v in enumerate(vectors):
-                lanes = slice(n * 128, n * 128 + 128)
-                for s, val in enumerate((y0 + o0, y1 + o1, y0 - o0, y1 - o1)):
-                    home[s, v, at, :] = val[:, lanes]
+        ya, yb = sums(ia, 0, ka), sums(ib, ka, kb)
+        y0, y1 = ya + yb, ya - yb
+        odd = sums(ic, ka + kb, kc)
+        o0, o1 = odd[:quarter], odd[quarter:]
+        for n, v in enumerate(vectors):
+            lanes = slice(n * 128, n * 128 + 128)
+            for s, val in enumerate((y0 + o0, y1 + o1, y0 - o0, y1 - o1)):
+                home[s, v] = val[:, lanes]
 
     def send(v):
         for p in (2, 1, 3):

time: 149 us -> 149 us (level)
  no operation moved by 1% of the time
where the time goes in v1:
time: 149 us
  Pallas kernels  144 us (97%)
  local copies, waits for them, and re-layouts  5.36 us (4%)
    pallas_call x1, Pallas kernels, local_waves(): pl.pallas_call(wave_kernel, out_shape=jax.ShapeDtypeStruct(prognostic.sha...  144 us
    unnamed x2, local copies, waits for them, and re-layouts  5.36 us

profile of v1, /device:TPU:9, one launch (start us, length us, event | category | flops | bytes accessed | tf_op | source)
XLA Modules:
  0.0 149.3 jit_solution(12353162941505827626)
XLA Ops:
  0.0 1.3 copy.15.kappa_ref
  1.3 143.9 %waves.1 = f32[6,2,576,128]{3,2,1,0:T(8,128)} custom-call(f32[6,2,576,128]{3,2,1,0:T(8,128)} %x_ref.1, f32[2,128]{1,0:T(2,128)} %wz_ref.1, f32[2,128]{1,0:T(2,128)} %wm_ref.1, f32[2]{0:T(128)} %depth_ref.1, f32[3,2]{1,0:T(4,128)} %copy.15.kappa_ref, f32[8,8,128]{2,1,0:T(8,128)} %constant.24.clone.gm_ref, f32[8,8,128]{2,1,0:T(8,128)} %constant.25.clone.ge_ref, ...), custom_call_target="tpu_custom_call" | custom-call | tf_op jit(solution)/shard_map/waves/pallas_call | solution.py:664
  145.2 4.0 %copy.17 = f32[6,2,576,128]{3,2,1,0:T(8,128)} copy(f32[6,2,576,128]{3,2,1,0:T(8,128)} %waves.1) | data formatting | bytes 7077888
